TPU v7x, 1024 devices: a whole 4x8x16 slice. The times are simulated.
1024 devices in a mesh: pipe: 2 (over x_lo), row: 32 (over z, core), col: 16 (over y, x_hi).
Axes of the slice: x: 4 (x_hi: 2, x_lo: 2; x = x_hi * 2 + x_lo), y: 8, z: 16, core: 2. Of those that a mesh axis runs over, the one named last changes fastest.
Arguments:
- grad_output: bfloat16 [4096, 4096], P('row', 'col'), may hold values from -6 to 6
- queries: bfloat16 [2, 4096, 4096], P('pipe', 'row', 'col'), may hold values from -70 to 70
- keys: bfloat16 [2, 4096, 4096], P('pipe', 'row', 'col'), may hold values from -8 to 8
- values: bfloat16 [2, 4096, 4096], P('pipe', 'row', 'col'), may hold values from -6 to 6
- value_weight: bfloat16 [2, 4096, 4096], P('pipe', 'col', 'row'), may hold values from -0.375 to 0.375
- random_table: int32 [2, 64, 32, 3], P('pipe', None, 'col'), may hold values from 0 to 63, as said below
Outputs:
- input_grads: bfloat16 [2, 4096, 4096], P('pipe', 'row', 'col')
- query_grads: bfloat16 [2, 4096, 4096], P('pipe', 'row', 'col')
- key_grads: bfloat16 [2, 4096, 4096], P('pipe', 'row', 'col')
Inputs may be any that keep to these rules, and one draw needn't show every extreme that they name: `random_table`: for each section, the random blocks that one aligned group of 2 query blocks names for one aligned group of 2 heads fall at most 1 times into any one aligned group of 2 key blocks, and exactly 1 times into some group.
All inputs are finite; a program needn't handle non-finite values.
Results may differ from a plain program's by a relative error of at most 0.03.
Values may be sent and summed in bfloat16 or wider, within the bound.
A program may use at most 32 MiB of HBM per device.

v0:
```python
import math

import jax
import jax.numpy as jnp
from jax import lax
from jax.sharding import PartitionSpec as P

HEAD_DIM = 128
BLOCK = 64
RANDOMS = 3


def padded(cells, sides, width):
    for axis, dim in sides:
        count = lax.axis_size(axis)
        ends = count - 1
        head = lax.slice_in_dim(cells, 0, width, axis=dim)
        tail = lax.slice_in_dim(cells, cells.shape[dim] - width, cells.shape[dim], axis=dim)
        cells = jnp.concatenate(
            [
                lax.ppermute(tail, axis, [(i, (i + 1) % count) for i in range(ends)]),
                cells,
                lax.ppermute(head, axis, [((i + 1) % count, i) for i in range(ends)]),
            ],
            axis=dim,
        )
    return cells


def from_behind(block, axis, distance):
    devices = range(lax.axis_size(axis))
    route = [(i - distance, i) for i in devices if i - distance in devices]
    return lax.ppermute(block, axis, route)


def send_back(local_sum, rim_terms, far_terms, slot_tile, slot_filled):
    qblocks, heads_dev, channels, block, head_dim = local_sum.shape
    near = padded(rim_terms, (("row", 1),), BLOCK)
    from_left = near[:, :block].reshape(channels, block, heads_dev, head_dim).transpose(2, 0, 1, 3)
    from_right = (
        near[:, 3 * block :].reshape(channels, block, heads_dev, head_dim).transpose(2, 0, 1, 3)
    )
    returned = lax.all_to_all(far_terms, "row", split_axis=0, concat_axis=0, tiled=True)
    flat_back = returned.reshape(slot_tile.shape[0], channels * block * head_dim)
    targets = jnp.arange(qblocks * heads_dev, dtype=jnp.int32)
    selector = ((slot_tile[:, None] == targets[None, :]) & slot_filled[:, None]).astype(
        jnp.bfloat16
    )
    far_sum = jnp.einsum("sq,sx->qx", selector, flat_back, preferred_element_type=jnp.float32)
    total = local_sum + far_sum.reshape(qblocks, heads_dev, channels, block, head_dim)
    total = total.at[0].add(from_left.astype(jnp.float32))
    total = total.at[qblocks - 1].add(from_right.astype(jnp.float32))
    return total


def body(grad_output, queries, keys, values, value_weight, random_table):
    tokens, features = grad_output.shape
    heads_dev = features // HEAD_DIM
    qblocks = tokens // BLOCK
    rows = lax.axis_size("row")
    row_index = lax.axis_index("row")
    phases = lax.axis_size("pipe")
    phase_index = lax.axis_index("pipe")
    scale = 1.0 / math.sqrt(HEAD_DIM)
    query = queries[0]
    key = keys[0]
    value = values[0]
    table = random_table[0]
    weight_full = lax.all_gather(value_weight[0], "row", axis=1, tiled=True)
    per_dst = qblocks * heads_dev * RANDOMS
    slots = (per_dst + rows - 1) // rows
    table_dst = table.reshape(rows, per_dst)
    source_all = table_dst // qblocks
    position = jnp.arange(per_dst, dtype=jnp.int32)
    same = source_all[:, :, None] == source_all[:, None, :]
    earlier = position[None, :] < position[:, None]
    rank_all = jnp.sum((same & earlier[None]).astype(jnp.int32), axis=2)
    head_of_entry = position // RANDOMS % heads_dev
    local_tile = (
        jnp.clip(table_dst - row_index * qblocks, 0, qblocks - 1) * heads_dev
        + head_of_entry[None, :]
    )
    mine = source_all == row_index
    slot_ids = jnp.arange(slots, dtype=jnp.int32)
    hits = mine[:, None, :] & (rank_all[:, None, :] == slot_ids[None, :, None])
    slot_filled = jnp.any(hits, axis=2).reshape(-1)
    slot_tile = jnp.sum(jnp.where(hits, local_tile[:, None, :], 0), axis=2).reshape(-1)
    paired = jnp.stack([key, value])
    tile_stack = paired.reshape(2, qblocks, BLOCK, heads_dev, HEAD_DIM).transpose(1, 3, 0, 2, 4)
    tile_stack = tile_stack.reshape(qblocks * heads_dev, 2, BLOCK, HEAD_DIM)
    payload = jnp.where(
        slot_filled[:, None, None, None], tile_stack[slot_tile], jnp.zeros((), jnp.bfloat16)
    )
    arrived = lax.all_to_all(
        payload.reshape(rows, slots, 2, BLOCK, HEAD_DIM),
        "row",
        split_axis=0,
        concat_axis=0,
        tiled=True,
    )
    source_me = lax.dynamic_index_in_dim(source_all, row_index, 0, keepdims=False)
    rank_me = lax.dynamic_index_in_dim(rank_all, row_index, 0, keepdims=False)
    entry_slot = source_me * slots + rank_me
    fetched = arrived.reshape(rows * slots, 2, BLOCK, HEAD_DIM)[entry_slot]
    fetched = fetched.reshape(qblocks, heads_dev, RANDOMS, 2, BLOCK, HEAD_DIM)
    extended = padded(paired, (("row", 1),), BLOCK)
    ext_blocks = extended.reshape(2, qblocks + 2, BLOCK, heads_dev, HEAD_DIM)
    window = jnp.stack([ext_blocks[:, offset : offset + qblocks] for offset in range(3)], axis=2)
    window = window.transpose(1, 4, 2, 0, 3, 5)
    tiles = jnp.concatenate([window, fetched], axis=2)
    key_tiles = tiles[:, :, :, 0]
    value_tiles = tiles[:, :, :, 1]
    global_block = row_index * qblocks + jnp.arange(qblocks, dtype=jnp.int32)
    left_ok = global_block >= 1
    right_ok = global_block + 1 < rows * qblocks
    valid = jnp.concatenate(
        [
            left_ok[:, None],
            jnp.ones((qblocks, 1), bool),
            right_ok[:, None],
            jnp.ones((qblocks, RANDOMS), bool),
        ],
        axis=1,
    )
    query_tiles = query.reshape(qblocks, BLOCK, heads_dev, HEAD_DIM)
    scores = (
        jnp.einsum("nihd,nhtjd->nhitj", query_tiles, key_tiles, preferred_element_type=jnp.float32)
        * scale
    )
    scores = jnp.where(valid[:, None, None, :, None], scores, -1e30)
    top = jnp.max(scores, axis=(3, 4), keepdims=True)
    log_total = top + jnp.log(jnp.sum(jnp.exp(scores - top), axis=(3, 4), keepdims=True))
    probs = jnp.exp(scores - log_total)
    probs_low = probs.astype(jnp.bfloat16)
    outputs = jnp.einsum(
        "nhitj,nhtjd->nihd", probs_low, value_tiles, preferred_element_type=jnp.float32
    )

    def as_rows(block_sum):
        return block_sum.transpose(0, 2, 1, 3).reshape(tokens, features).astype(jnp.bfloat16)

    upstream = grad_output
    kept_input = jnp.zeros((tokens, features), jnp.bfloat16)
    kept_query = jnp.zeros((tokens, features), jnp.bfloat16)
    kept_key = jnp.zeros((tokens, features), jnp.bfloat16)
    for step in range(phases):
        active = phase_index == phases - 1 - step
        grad_tiles = upstream.reshape(qblocks, BLOCK, heads_dev, HEAD_DIM)
        delta = jnp.sum(grad_tiles.astype(jnp.float32) * outputs, axis=3)
        delta = delta.transpose(0, 2, 1)[:, :, :, None, None]
        dprobs = jnp.einsum(
            "nihd,nhtjd->nhitj", grad_tiles, value_tiles, preferred_element_type=jnp.float32
        )
        dscores = (probs * (dprobs - delta) * scale).astype(jnp.bfloat16)
        query_grad = jnp.einsum(
            "nhitj,nhtjd->nihd", dscores, key_tiles, preferred_element_type=jnp.float32
        )
        query_grad = query_grad.astype(jnp.bfloat16).reshape(tokens, features)
        key_terms = jnp.einsum(
            "nhitj,nihd->nhtjd", dscores, query_tiles, preferred_element_type=jnp.float32
        ).astype(jnp.bfloat16)
        value_terms = jnp.einsum(
            "nhitj,nihd->nhtjd", probs_low, grad_tiles, preferred_element_type=jnp.float32
        ).astype(jnp.bfloat16)
        terms = jnp.stack([key_terms, value_terms], axis=3)
        local_sum = terms[:, :, 1].astype(jnp.float32)
        local_sum = local_sum + jnp.pad(
            terms[1:, :, 0].astype(jnp.float32), ((0, 1), (0, 0), (0, 0), (0, 0), (0, 0))
        )
        local_sum = local_sum + jnp.pad(
            terms[:-1, :, 2].astype(jnp.float32), ((1, 0), (0, 0), (0, 0), (0, 0), (0, 0))
        )
        to_left = terms[0, :, 0]
        to_right = terms[qblocks - 1, :, 2]
        rim_terms = (
            jnp.concatenate([to_left, to_right], axis=2)
            .transpose(1, 2, 0, 3)
            .reshape(2, 2 * BLOCK, features)
        )
        far_list = terms[:, :, 3:].reshape(per_dst, 2, BLOCK, HEAD_DIM)
        far_terms = (
            jnp.zeros((rows * slots, 2, BLOCK, HEAD_DIM), jnp.bfloat16).at[entry_slot].set(far_list)
        )
        far_terms = far_terms.reshape(rows, slots, 2, BLOCK, HEAD_DIM)
        query_grad, local_sum, rim_terms, far_terms = (query_grad, local_sum, rim_terms, far_terms)
        total = send_back(local_sum, rim_terms, far_terms, slot_tile, slot_filled)
        kept_key = jnp.where(active, as_rows(total[:, :, 0]), kept_key)
        value_grad = as_rows(total[:, :, 1])
        summed = lax.dot_general(
            lax.all_gather(value_grad, "col", axis=1, tiled=True),
            weight_full,
            (((1,), (1,)), ((), ())),
            preferred_element_type=jnp.float32,
        )
        input_grad = (upstream.astype(jnp.float32) + summed).astype(jnp.bfloat16)
        kept_query = jnp.where(active, query_grad, kept_query)
        kept_input = jnp.where(active, input_grad, kept_input)
        if step + 1 < phases:
            upstream = from_behind(input_grad, "pipe", -1)
    return (kept_input[None], kept_query[None], kept_key[None])


def solution(mesh):
    in_specs = (
        P("row", "col"),
        P("pipe", "row", "col"),
        P("pipe", "row", "col"),
        P("pipe", "row", "col"),
        P("pipe", "col", "row"),
        P("pipe", None, "col", None),
    )
    out_specs = (P("pipe", "row", "col"), P("pipe", "row", "col"), P("pipe", "row", "col"))
    return jax.shard_map(body, mesh=mesh, in_specs=in_specs, out_specs=out_specs, check_vma=False)
```

profile of v0, /device:TPU:2, one launch (start us, length us, event | category | flops | bytes accessed | tf_op | source)
XLA Modules:
  0.0 461.2 jit_solution(10876863311116075016)
XLA Ops:
  7.2 0.8 copy.285
  8.0 0.1 reshape_squeeze.9
  8.1 0.1 reshape_squeeze.8
  8.4 0.1 convert_reduce_fusion
  8.7 0.8 constant_dynamic-update-slice_fusion.1
  9.5 0.8 constant_dynamic-update-slice_fusion
  10.4 0.7 gather_fusion
  11.2 1.1 fusion.32
  12.3 19.1 %all-to-all-start = ((bf16[32,1,2,64,128]{4,3,2,1,0:T(8,128)(2,1)}), bf16[32,1,2,64,128]{4,3,2,1,0:T(8,128)(2,1)S(1)}, u32[]{:S(2)}, u32[]{:S(2)}) async-start(bf16[32,1,2,64,128]{4,3,2,1,0:T(8,128)(2,1)} %fusion.32), calls=%async_computation | async-start | bytes 2097152 | tf_op jit(solution)/shard_map/all_to_all | solution.py:94
  31.5 2.2 collective-permute-start
  33.7 1.3 collective-permute-start.1
  35.2 0.2 add_reduce_fusion
  35.5 2.5 collective-permute-done.1
  38.1 0.3 fusion.107
  38.5 49.4 %all-to-all-done = bf16[32,1,2,64,128]{4,3,2,1,0:T(8,128)(2,1)S(1)} async-done(((bf16[32,1,2,64,128]{4,3,2,1,0:T(8,128)(2,1)}), bf16[32,1,2,64,128]{4,3,2,1,0:T(8,128)(2,1)S(1)}, u32[]{:S(2)}, u32[]{:S(2)}) %all-to-all-start) | async-done | bytes 1048608 | tf_op jit(solution)/shard_map/all_to_all | solution.py:94
  87.9 0.6 gather_fusion.1
  88.6 0.3 fusion.111
  88.9 0.1 exponential_reduce_fusion
  89.0 0.1 fusion.35
  89.2 0.4 multiply_reduce_fusion.1
  89.5 0.2 fusion.14
  89.8 0.3 fusion.11
  90.1 0.2 fusion.13
  90.4 0.4 copy-done.1
  90.8 1.2 broadcast_in_dim.34.clone
  92.1 2.5 scatter_fusion
  94.6 4.7 %all-to-all-start.1 = ((bf16[32,1,2,64,128]{4,3,2,1,0:T(8,128)(2,1)}), bf16[32,1,2,64,128]{4,3,2,1,0:T(8,128)(2,1)}, u32[]{:S(2)}, u32[]{:S(2)}) async-start(bf16[32,1,2,64,128]{4,3,2,1,0:T(8,128)(2,1)} %bitcast.297), calls=%async_computation.1 | async-start | bytes 2097152 | tf_op jit(solution)/shard_map/all_to_all | solution.py:43
  99.3 0.7 all-gather.9.cloned.1.call-update
  100.1 0.1 copy.312
  100.4 2.0 collective-permute-start.2
  102.6 1.3 collective-permute-start.3
  103.9 53.0 %all-to-all-done.1 = bf16[32,1,2,64,128]{4,3,2,1,0:T(8,128)(2,1)} async-done(((bf16[32,1,2,64,128]{4,3,2,1,0:T(8,128)(2,1)}), bf16[32,1,2,64,128]{4,3,2,1,0:T(8,128)(2,1)}, u32[]{:S(2)}, u32[]{:S(2)}) %all-to-all-start.1) | async-done | bytes 1048608 | tf_op jit(solution)/shard_map/all_to_all | solution.py:43
  156.8 1.9 copy.441
  158.7 0.2 copy.389
  159.0 0.7 fusion.30
  160.0 0.6 copy.444
  160.6 33.7 %all-gather.9.cloned.1.call-done = bf16[1,256,4096]{2,1,0:T(8,128)(2,1)} async-done(((bf16[1,256,128]{2,1,0:T(8,128)(2,1)}), bf16[1,256,4096]{2,1,0:T(8,128)(2,1)}) %all-gather.9.cloned.1.call-update) | async-done | bytes 2097168 | tf_op jit(solution)/shard_map/all_gather | solution.py:69
  194.3 92.5 %all-gather.5.cloned.1.call-done = bf16[128,4096]{1,0:T(8,128)(2,1)} async-done(((bf16[128,256]{1,0:T(8,128)(2,1)}), bf16[128,4096]{1,0:T(8,128)(2,1)}) %all-gather.5.cloned.1.call-update) | async-done | bytes 1048592 | tf_op jit(solution)/shard_map/all_gather | solution.py:190
  286.9 2.8 fusion.20
  289.6 3.4 collective-permute-start.4
  293.0 1.9 collective-permute-done.4
  295.0 0.5 copy-done.8
  295.5 0.2 fusion.16
  295.8 0.3 fusion.12
  296.1 0.8 copy-done.3
  296.8 0.2 fusion.15
  297.2 1.2 broadcast_in_dim.34
  298.4 2.5 scatter_fusion.1
  300.9 13.3 %all-to-all-start.2 = ((bf16[32,1,2,64,128]{4,3,2,1,0:T(8,128)(2,1)}), bf16[32,1,2,64,128]{4,3,2,1,0:T(8,128)(2,1)S(1)}, u32[]{:S(2)}, u32[]{:S(2)}) async-start(bf16[32,1,2,64,128]{4,3,2,1,0:T(8,128)(2,1)} %bitcast.62), calls=%async_computation.2 | async-start | bytes 2097152 | tf_op jit(solution)/shard_map/all_to_all | solution.py:43
  314.4 0.1 copy.330
  314.7 2.2 collective-permute-start.5
  317.0 1.5 collective-permute-start.6
  318.5 52.2 %all-to-all-done.2 = bf16[32,1,2,64,128]{4,3,2,1,0:T(8,128)(2,1)S(1)} async-done(((bf16[32,1,2,64,128]{4,3,2,1,0:T(8,128)(2,1)}), bf16[32,1,2,64,128]{4,3,2,1,0:T(8,128)(2,1)S(1)}, u32[]{:S(2)}, u32[]{:S(2)}) %all-to-all-start.2) | async-done | bytes 1048608 | tf_op jit(solution)/shard_map/all_to_all | solution.py:43
  370.7 0.7 copy.440
  371.4 0.2 copy.392
  371.6 0.7 fusion.28
  372.5 0.6 fusion.67
  373.2 0.6 copy.443
  373.9 1.3 fusion.23
  375.2 0.3 fusion.27
  375.6 0.7 select_n.219
  376.3 0.7 select_n.226
  377.0 75.0 %all-gather.7.cloned.1.call-done = bf16[128,4096]{1,0:T(8,128)(2,1)} async-done(((bf16[128,256]{1,0:T(8,128)(2,1)}), bf16[128,4096]{1,0:T(8,128)(2,1)}) %all-gather.7.cloned.1.call-update) | async-done | bytes 1048592 | tf_op jit(solution)/shard_map/all_gather | solution.py:190
  452.0 2.7 fusion.65
  (93 shorter events, 2.6 us)
Async XLA Ops:
  11.2 24.0 %copy-start.11 = (bf16[1,128,256]{2,1,0:T(8,128)(2,1)S(1)}, bf16[1,128,256]{2,1,0:T(8,128)(2,1)}, u32[]{:S(2)}) copy-start(bf16[1,128,256]{2,1,0:T(8,128)(2,1)} %param.15) | copy-start | bytes 196612
  11.2 24.0 %copy-start.6 = (bf16[128,256]{1,0:T(8,128)(2,1)S(1)}, bf16[128,256]{1,0:T(8,128)(2,1)}, u32[]{:S(2)}) copy-start(bf16[128,256]{1,0:T(8,128)(2,1)} %param.14) | copy-start | bytes 196612
  12.3 75.6 %all-to-all-start = ((bf16[32,1,2,64,128]{4,3,2,1,0:T(8,128)(2,1)}), bf16[32,1,2,64,128]{4,3,2,1,0:T(8,128)(2,1)S(1)}, u32[]{:S(2)}, u32[]{:S(2)}) async-start(bf16[32,1,2,64,128]{4,3,2,1,0:T(8,128)(2,1)} %fusion.32), calls=%async_computation | async-start | bytes 2097152 | tf_op jit(solution)/shard_map/all_to_all | solution.py:94
  31.5 4.0 collective-permute-start
  33.7 4.3 collective-permute-start.1
  90.1 0.7 copy-start.1
  94.6 62.3 %all-to-all-start.1 = ((bf16[32,1,2,64,128]{4,3,2,1,0:T(8,128)(2,1)}), bf16[32,1,2,64,128]{4,3,2,1,0:T(8,128)(2,1)}, u32[]{:S(2)}, u32[]{:S(2)}) async-start(bf16[32,1,2,64,128]{4,3,2,1,0:T(8,128)(2,1)} %bitcast.297), calls=%async_computation.1 | async-start | bytes 2097152 | tf_op jit(solution)/shard_map/all_to_all | solution.py:43
  99.2 95.1 %all-gather.9.cloned.1.call-start = ((), (), s32[]{:S(2)}) async-start(), calls=%async_computation.5 | async-start | bytes 2162688 | tf_op jit(solution)/shard_map/all_gather | solution.py:69
  100.0 186.9 %all-gather.5.cloned.1.call-start = ((), (), s32[]{:S(2)}) async-start(), calls=%async_computation.3 | async-start | bytes 1114112 | tf_op jit(solution)/shard_map/all_gather | solution.py:190
  100.0 59.0 %copy-start.12 = (s32[2,2]{1,0:T(2,128)}, s32[2,2]{1,0:T(2,128)S(1)}, u32[]{:S(2)}) copy-start(s32[2,2]{1,0:T(2,128)S(1)} %multiply_add_fusion) | copy-start | bytes 52
  100.4 59.3 %collective-permute-start.2 = (bf16[2,64,256]{2,1,0:T(8,128)(2,1)S(1)}, bf16[2,64,256]{2,1,0:T(8,128)(2,1)S(1)}, u32[]{:S(2)}, u32[]{:S(2)}) collective-permute-start(bf16[2,64,256]{2,1,0:T(8,128)(2,1)S(1)} %copy.379), channel_id=1, source_target_pairs={{0,16},{16,32},{32,48},{48,64},{64,80},{80,96},{96,112},{112,128},... | collective-permute-start | bytes 196616 | tf_op jit(solution)/shard_map/ppermute | solution.py:21
  102.6 57.2 %collective-permute-start.3 = (bf16[2,64,256]{2,1,0:T(8,128)(2,1)S(1)}, bf16[2,64,256]{2,1,0:T(8,128)(2,1)S(1)}, u32[]{:S(2)}, u32[]{:S(2)}) collective-permute-start(bf16[2,64,256]{2,1,0:T(8,128)(2,1)S(1)} %copy.380), channel_id=1, source_target_pairs={{16,0},{32,16},{48,32},{64,48},{80,64},{96,80},{112,96},{128,112},... | collective-permute-start | bytes 196616 | tf_op jit(solution)/shard_map/ppermute | solution.py:23
  159.0 127.9 %copy-start.7 = (bf16[128,256]{1,0:T(8,128)(2,1)S(1)}, bf16[128,256]{1,0:T(8,128)(2,1)}, u32[]{:S(2)}) copy-start(bf16[128,256]{1,0:T(8,128)(2,1)} %param.14) | copy-start | bytes 196612
  289.6 7.5 %copy-start.4 = (bf16[128,256]{1,0:T(8,128)(2,1)}, bf16[128,256]{1,0:T(8,128)(2,1)S(1)}, u32[]{:S(2)}) copy-start(bf16[128,256]{1,0:T(8,128)(2,1)S(1)} %fusion.20) | copy-start | bytes 196612
  289.6 5.3 %collective-permute-start.4 = (bf16[128,256]{1,0:T(8,128)(2,1)S(1)}, bf16[128,256]{1,0:T(8,128)(2,1)S(1)}, u32[]{:S(2)}, u32[]{:S(2)}) collective-permute-start(bf16[128,256]{1,0:T(8,128)(2,1)S(1)} %fusion.20), channel_id=1, source_target_pairs={{512,0},{513,1},{514,2},{515,3},{516,4},{517,5},{518,6},{519,7},{5... | collective-permute-start | bytes 196616 | tf_op jit(solution)/shard_map/ppermute | solution.py:33
  294.9 0.6 copy-start.8
  296.0 0.8 copy-start.3
  300.9 69.8 %all-to-all-start.2 = ((bf16[32,1,2,64,128]{4,3,2,1,0:T(8,128)(2,1)}), bf16[32,1,2,64,128]{4,3,2,1,0:T(8,128)(2,1)S(1)}, u32[]{:S(2)}, u32[]{:S(2)}) async-start(bf16[32,1,2,64,128]{4,3,2,1,0:T(8,128)(2,1)} %bitcast.62), calls=%async_computation.2 | async-start | bytes 2097152 | tf_op jit(solution)/shard_map/all_to_all | solution.py:43
  314.2 137.7 %all-gather.7.cloned.1.call-start = ((), (), s32[]{:S(2)}) async-start(), calls=%async_computation.4 | async-start | bytes 1114112 | tf_op jit(solution)/shard_map/all_gather | solution.py:190
  314.7 57.6 %collective-permute-start.5 = (bf16[2,64,256]{2,1,0:T(8,128)(2,1)S(1)}, bf16[2,64,256]{2,1,0:T(8,128)(2,1)S(1)}, u32[]{:S(2)}, u32[]{:S(2)}) collective-permute-start(bf16[2,64,256]{2,1,0:T(8,128)(2,1)S(1)} %copy.382), channel_id=1, source_target_pairs={{0,16},{16,32},{32,48},{48,64},{64,80},{80,96},{96,112},{112,128},... | collective-permute-start | bytes 196616 | tf_op jit(solution)/shard_map/ppermute | solution.py:21
  317.0 55.4 %collective-permute-start.6 = (bf16[2,64,256]{2,1,0:T(8,128)(2,1)S(1)}, bf16[2,64,256]{2,1,0:T(8,128)(2,1)S(1)}, u32[]{:S(2)}, u32[]{:S(2)}) collective-permute-start(bf16[2,64,256]{2,1,0:T(8,128)(2,1)S(1)} %copy.383), channel_id=1, source_target_pairs={{16,0},{32,16},{48,32},{64,48},{80,64},{96,80},{112,96},{128,112},... | collective-permute-start | bytes 196616 | tf_op jit(solution)/shard_map/ppermute | solution.py:23
  370.7 0.9 copy-start.13
  372.3 2.9 copy-start.2
  372.5 79.5 %copy-start = (bf16[1,256,4096]{2,1,0:T(8,128)(2,1)S(1)}, bf16[1,256,4096]{2,1,0:T(8,128)(2,1)}, u32[]{:S(2)}) copy-start(bf16[1,256,4096]{2,1,0:T(8,128)(2,1)} %all-gather.9.cloned.1.call-done) | copy-start | bytes 6291460
  373.1 3.1 copy-start.10
  373.1 78.8 %copy-start.5 = (bf16[128,256]{1,0:T(8,128)(2,1)S(1)}, bf16[128,256]{1,0:T(8,128)(2,1)}, u32[]{:S(2)}) copy-start(bf16[128,256]{1,0:T(8,128)(2,1)} %copy-done.4) | copy-start | bytes 196612
  373.1 78.8 %copy-start.9 = (bf16[128,256]{1,0:T(8,128)(2,1)S(1)}, bf16[128,256]{1,0:T(8,128)(2,1)}, u32[]{:S(2)}) copy-start(bf16[128,256]{1,0:T(8,128)(2,1)} %copy-done.8) | copy-start | bytes 196612
Sparse Core Ops, SparseCore 0:
  102.7 91.5 all-gather.8
  199.1 87.6 all-gather.4
  374.0 77.9 all-gather.6
where the time goes:
time: 463 us; the launch traced here: 461 us
  waiting for transfers between devices  361 us (78%)
  starting transfers between devices  51.1 us (11%)
  local copies, waits for them, and re-layouts  21.1 us (5%)
  between operations  14.5 us (3%)
  matrix products  10.6 us (2%)
    all_gather x2, waiting for transfers between devices, body(): lax.all_gather(value_grad, 'col', axis=1, tiled=True)  168 us
    all_to_all x2, waiting for transfers between devices, send_back(): lax.all_to_all(far_terms, 'row', split_axis=0, concat_axis=0, tiled=True)  105 us
    all_to_all x1, waiting for transfers between devices, body(): lax.all_to_all(payload.reshape(rows, slots, 2, BLOCK, HEAD_DIM), 'row', s...  49.4 us
    all_gather x1, waiting for transfers between devices, body(): weight_full = lax.all_gather(value_weight[0], 'row', axis=1, tiled=True)  33.7 us
    all_to_all x1, starting transfers between devices, body(): lax.all_to_all(payload.reshape(rows, slots, 2, BLOCK, HEAD_DIM), 'row', s...  19.1 us
    all_to_all x2, starting transfers between devices, send_back(): lax.all_to_all(far_terms, 'row', split_axis=0, concat_axis=0, tiled=True)  18 us
  transfers between devices with their start and end apart: 13, of which 8 were waited for; matrix products, arithmetic and copies ran while one was open for 2% of the time, Pallas kernels for 0%

commit v1 on v0

v1 whole, which is shorter than its diff:
```python
import math

import jax
import jax.numpy as jnp
from jax import lax
from jax.experimental import pallas as pl
from jax.experimental.pallas import tpu as pltpu
from jax.sharding import PartitionSpec as P

HEAD_DIM = 128
BLOCK = 64
RANDOMS = 3
HEADS_DEV = 2
QBLOCKS = 2
TILES = 3 + RANDOMS
ENTRIES = QBLOCKS * RANDOMS
ZERO, RIM_LEFT, RIM_RIGHT, SLOTS = ENTRIES, ENTRIES + 1, ENTRIES + 2, ENTRIES + 3
MESH = pl.DeviceIdType.MESH
BF16 = jnp.bfloat16
F32 = jnp.float32


def drive(*streams):
    streams = list(streams)
    while streams:
        for stream in list(streams):
            if next(stream, "end") == "end":
                streams.remove(stream)


def lanes(head):
    return pl.ds(head * HEAD_DIM, HEAD_DIM)


def kernel(
    rows,
    cols,
    table,
    grad,
    query,
    key,
    value,
    weight,
    input_out,
    query_out,
    key_out,
    key_all,
    value_all,
    weight_all,
    grad_all,
    up,
    probs,
    acc,
    v_own,
    v_sib,
    v_local,
    v_send,
    v_recv,
    k_own,
    k_sib,
    k_local,
    k_send,
    k_recv,
    ring_send,
    ring_recv,
    sib_send,
    sib_recv,
    col_send,
    col_recv,
    sum_send,
    sum_recv,
    one_send,
    one_recv,
):
    chips = rows // 2
    ycount = cols // 2
    scale = 1.0 / math.sqrt(HEAD_DIM)
    pipe = lax.axis_index("pipe")
    row = lax.axis_index("row")
    col = lax.axis_index("col")
    chip, core = row // 2, lax.rem(row, 2)
    ypos, xpos = col // 2, lax.rem(col, 2)
    sibling = row + 1 - 2 * core
    row_next = ({"row": lax.rem(row + 2, rows)}, {"row": lax.rem(row + rows - 2, rows)})
    col_next = ({"col": lax.rem(col + 2, cols)}, {"col": lax.rem(col + cols - 2, cols)})
    to_sibling = {"row": sibling}
    to_partner = {"col": col + 1 - 2 * xpos}
    to_pipe = {"pipe": 1 - pipe}

    barrier = pltpu.get_barrier_semaphore()
    for device in (*row_next, *col_next, to_sibling, to_partner, to_pipe):
        pl.semaphore_signal(barrier, inc=1, device_id=device, device_id_type=MESH)
    pl.semaphore_wait(barrier, 7)

    def remote(src, dst, send, recv, device):
        return pltpu.make_async_remote_copy(
            src_ref=src,
            dst_ref=dst,
            send_sem=send,
            recv_sem=recv,
            device_id=device,
            device_id_type=MESH,
        )

    def gather(sent, buf, pos, size, entry, devices, send, recv, shared=None, second=None, arrive=None):
        half = size // 2

        def ref(offset, item):
            return buf.at[entry(lax.rem(pos + offset + size, size), item)]

        def copy(way, step, item):
            offset = step if way else -step
            return remote(
                ref(offset, item),
                ref(offset, item),
                send.at[way, step, item],
                recv.at[way, step, item],
                devices[way],
            )

        def push(way, step, item):
            if step < half - 1 or (step == half - 1 and way == item):
                made = copy(way, step, item)
                made.start()
                sent.append(made)

        def arrived(way, step, item):
            offset = step if way else -step
            remote(
                ref(offset, item),
                ref(offset, item),
                send.at[way, step - 1, item],
                recv.at[way, step - 1, item],
                devices[way],
            ).wait_recv()

        def share(offset):
            if shared is not None:
                shared(offset)

        for item in range(2):
            if item == 1 and second is not None:
                second()
            for way in range(2):
                push(way, 0, item)
        share(0)
        if arrive is not None:
            arrive(0, 0)
            arrive(0, 1)
        yield
        for step in range(1, half):
            for item in range(2):
                for way in range(2):
                    arrived(way, step, item)
                    push(way, step, item)
                if item == 1:
                    share(-step)
                    share(step)
                if arrive is not None:
                    arrive(-step, item)
                    arrive(step, item)
                yield
        for way in range(2):
            arrived(way, half, way)
        share(half)
        if arrive is not None:
            arrive(half, 0)
            arrive(half, 1)
        yield

    def row_gather(sent, which, buf):
        shares = []

        def entry(place, item):
            return 4 * place + 2 * core + item

        def shared(offset):
            place = lax.rem(chip + offset + chips, chips)
            block = buf.at[pl.ds(4 * place + 2 * core, 2)]
            slot = (offset + chips) % chips
            made = remote(
                block, block, sib_send.at[which, slot], sib_recv.at[which, slot], to_sibling
            )
            made.start()
            shares.append(made)

        yield from gather(
            sent,
            buf,
            chip,
            chips,
            entry,
            row_next,
            ring_send.at[which],
            ring_recv.at[which],
            shared=shared,
        )
        for made in shares:
            made.wait_recv()
        sent.extend(shares)

    def tile_ids(n, head):
        block = 2 * row + n
        ids = [
            lax.rem(block + 2 * rows - 1, 2 * rows),
            block,
            lax.rem(block + 1, 2 * rows),
        ]
        for t in range(RANDOMS):
            ids.append(table[row * 12 + n * 6 + head * 3 + t])
        return ids

    def tiles(buf, n, head):
        return jnp.concatenate([buf[i, :, lanes(head)] for i in tile_ids(n, head)], axis=0)

    def rows_of(ref, n, head):
        return ref[pl.ds(n * BLOCK, BLOCK), lanes(head)]

    def make_probs():
        for n in range(QBLOCKS):
            for head in range(HEADS_DEV):
                scores = scale * lax.dot_general(
                    rows_of(query, n, head),
                    tiles(key_all, n, head),
                    (((1,), (1,)), ((), ())),
                    preferred_element_type=F32,
                )
                place = lax.broadcasted_iota(jnp.int32, scores.shape, 1) // BLOCK
                block = 2 * row + n
                gone = jnp.where(block == 0, 0, -1)
                gone_right = jnp.where(block == 2 * rows - 1, 2, -1)
                scores = jnp.where((place == gone) | (place == gone_right), -1e30, scores)
                top = jnp.max(scores, axis=1, keepdims=True)
                total = jnp.sum(jnp.exp(scores - top), axis=1, keepdims=True)
                probs[n, head] = jnp.exp(scores - (top + jnp.log(total)))

    def keep_terms(n, head, terms, own, local):
        terms = terms.astype(BF16)
        part = [terms[t * BLOCK : (t + 1) * BLOCK] for t in range(TILES)]
        for t in range(RANDOMS):
            own[head * SLOTS + n * RANDOMS + t] = part[3 + t]
        if n == 0:
            own[head * SLOTS + ZERO] = jnp.zeros_like(part[0])
            own[head * SLOTS + RIM_LEFT] = part[0]
            local[0, :, lanes(head)] = part[1].astype(F32)
            local[1, :, lanes(head)] = part[2].astype(F32)
        else:
            local[0, :, lanes(head)] += part[0].astype(F32)
            local[1, :, lanes(head)] += part[1].astype(F32)
            own[head * SLOTS + RIM_RIGHT] = part[2]

    def transposed_dot(left, right):
        return lax.dot_general(left, right, (((0,), (0,)), ((), ())), preferred_element_type=F32)

    def value_terms():
        for n in range(QBLOCKS):
            for head in range(HEADS_DEV):
                low = probs[n, head].astype(BF16)
                keep_terms(n, head, transposed_dot(low, rows_of(up, n, head)), v_own, v_local)

    def key_terms():
        for n in range(QBLOCKS):
            for head in range(HEADS_DEV):
                prob = probs[n, head]
                dprobs = lax.dot_general(
                    rows_of(up, n, head),
                    tiles(value_all, n, head),
                    (((1,), (1,)), ((), ())),
                    preferred_element_type=F32,
                )
                low = prob.astype(BF16).astype(F32)
                delta = jnp.sum(low * dprobs, axis=1, keepdims=True)
                dscores = (prob * (dprobs - delta) * scale).astype(BF16)
                query_out[pl.ds(n * BLOCK, BLOCK), lanes(head)] = jnp.dot(
                    dscores, tiles(key_all, n, head), preferred_element_type=F32
                ).astype(BF16)
                keep_terms(
                    n, head, transposed_dot(dscores, rows_of(query, n, head)), k_own, k_local
                )
                yield

    def find(owner, block, head):
        found = ZERO
        for n in range(QBLOCKS):
            for t in range(RANDOMS):
                named = table[owner * 12 + n * 6 + head * 3 + t]
                found = jnp.where(named == block, n * RANDOMS + t, found)
        return found

    def reduce(sent, which, own, sib, local, sbuf, rbuf, result):
        half = chips // 2

        def contribution(offset, part, head):
            place = lax.rem(chip + offset + chips, chips)
            block = 4 * place + 2 * core + part
            found = own[head * SLOTS + find(row, block, head)].astype(F32)
            found += sib[head * SLOTS + find(sibling, block, head)].astype(F32)
            rim = None
            if (offset, part) == (0, 0):
                rim = jnp.where(core == 1, RIM_RIGHT, ZERO)
            if (offset, part) == (0, 1):
                rim = jnp.where(core == 0, RIM_LEFT, ZERO)
            if (offset, part) == (1, 0):
                rim = jnp.where(core == 0, RIM_RIGHT, ZERO)
            if (offset, part) == (-1, 1):
                rim = jnp.where(core == 1, RIM_LEFT, ZERO)
            if rim is not None:
                found += sib[head * SLOTS + rim].astype(F32)
            return found

        def copy(way, step, part):
            return remote(
                sbuf.at[way, step, part],
                rbuf.at[way, step, part],
                sum_send.at[which, way, step, part],
                sum_recv.at[which, way, step, part],
                row_next[way],
            )

        exchange = remote(own, sib, one_send.at[which], one_recv.at[which], to_sibling)
        exchange.start()
        exchange.wait_recv()
        sent.append(exchange)
        for step in range(half):
            for part in range(2):
                for way in range(2):
                    if step == 0 and part != way:
                        continue
                    distance = half - step
                    offset = -distance if way else distance
                    terms = [contribution(offset, part, head) for head in range(HEADS_DEV)]
                    if step > 1 or (step == 1 and part == way):
                        copy(way, step - 1, part).wait_recv()
                        for head in range(HEADS_DEV):
                            terms[head] += rbuf[way, step - 1, part, :, lanes(head)].astype(F32)
                    for head in range(HEADS_DEV):
                        sbuf[way, step, part, :, lanes(head)] = terms[head].astype(BF16)
                    made = copy(way, step, part)
                    made.start()
                    sent.append(made)
                yield
        for part in range(2):
            total = local[part] + jnp.concatenate(
                [contribution(0, part, head) for head in range(HEADS_DEV)], axis=1
            )
            for way in range(2):
                copy(way, half - 1, part).wait_recv()
                total += rbuf[way, half - 1, part].astype(F32)
            result(part, total.astype(BF16))
        yield

    def keep_value_grad(part, total):
        grad_all[col, pl.ds(part * BLOCK, BLOCK)] = total

    def keep_key_grad(part, total):
        key_out[pl.ds(part * BLOCK, BLOCK)] = total

    def col_entry(place, item):
        own = 2 * place + xpos
        return own if item == 0 else 2 * place + 1 - xpos

    def project(place):
        total = acc[...]
        for part in range(2):
            total += lax.dot_general(
                grad_all[place, :, lanes(part)],
                weight_all[pl.ds(4 * place + 2 * part, 2)].reshape(2 * HEAD_DIM, HEAD_DIM),
                (((1,), (1,)), ((), ())),
                preferred_element_type=F32,
            )
        acc[...] = total

    def col_gather(sent, arrive):
        def exchange():
            return remote(
                grad_all.at[col], grad_all.at[col], one_send.at[2], one_recv.at[2], to_partner
            )

        made = exchange()
        made.start()
        sent.append(made)

        def on_arrive(offset, item):
            if arrive:
                project(col_entry(lax.rem(ypos + offset + ycount, ycount), item))

        yield from gather(
            sent,
            grad_all,
            ypos,
            ycount,
            col_entry,
            col_next,
            col_send,
            col_recv,
            second=lambda: exchange().wait_recv(),
            arrive=on_arrive,
        )

    def upstream_copy():
        return remote(input_out, up, one_send.at[3], one_recv.at[3], to_pipe)

    def key_reduce(sent):
        yield from reduce(sent, 1, k_own, k_sib, k_local, k_send, k_recv, keep_key_grad)

    def value_reduce(sent):
        yield from reduce(sent, 0, v_own, v_sib, v_local, v_send, v_recv, keep_value_grad)

    own_rows = pl.ds(2 * row, 2)
    key_all[own_rows] = key[...].reshape(2, BLOCK, key.shape[1])
    value_all[own_rows] = value[...].reshape(2, BLOCK, value.shape[1])
    weight_all[own_rows] = weight[...].reshape(2, HEAD_DIM, HEAD_DIM)

    @pl.when(pipe == 1)
    def _():
        sent = []
        drive(row_gather(sent, 0, key_all))
        make_probs()
        up[...] = grad[...]
        value_terms()
        drive(value_reduce(sent))
        acc[...] = up[...].astype(F32)
        drive(col_gather(sent, False), row_gather(sent, 1, weight_all))

        def step(place, carry):
            project(place)
            return carry

        lax.fori_loop(0, cols, step, 0)
        input_out[...] = acc[...].astype(BF16)
        made = upstream_copy()
        made.start()
        drive(row_gather(sent, 2, value_all))
        drive(key_terms())
        drive(key_reduce(sent))
        made.wait_send()
        for made in sent:
            made.wait_send()

    @pl.when(pipe == 0)
    def _():
        sent = []
        drive(row_gather(sent, 0, key_all))
        make_probs()
        drive(row_gather(sent, 1, weight_all))
        drive(row_gather(sent, 2, value_all))
        upstream_copy().wait_recv()
        value_terms()
        drive(value_reduce(sent), key_terms())
        acc[...] = up[...].astype(F32)
        drive(col_gather(sent, True), key_reduce(sent))
        input_out[...] = acc[...].astype(BF16)
        for made in sent:
            made.wait_send()


def body(grad_output, queries, keys, values, value_weight, random_table):
    rows = lax.axis_size("row")
    cols = lax.axis_size("col")
    tokens, features = grad_output.shape
    chips, ycount = rows // 2, cols // 2
    vmem = pl.BlockSpec(memory_space=pltpu.VMEM)
    dma = pltpu.SemaphoreType.DMA
    out = jax.ShapeDtypeStruct((tokens, features), BF16)
    ring = (2, chips // 2, 2, BLOCK, features)
    terms = (HEADS_DEV * SLOTS, BLOCK, HEAD_DIM)
    reducing = [
        pltpu.VMEM(terms, BF16),
        pltpu.VMEM(terms, BF16),
        pltpu.VMEM((2, BLOCK, features), F32),
        pltpu.VMEM(ring, BF16),
        pltpu.VMEM(ring, BF16),
    ]

    def run(*refs):
        kernel(rows, cols, *refs)

    flops = 10 * 2 * tokens * features * TILES * BLOCK + 2 * tokens * features * cols * features
    grads = pl.pallas_call(
        run,
        out_shape=(out, out, out),
        in_specs=[pl.BlockSpec(memory_space=pltpu.SMEM)] + [vmem] * 5,
        out_specs=(vmem, vmem, vmem),
        scratch_shapes=[
            pltpu.VMEM((2 * rows, BLOCK, features), BF16),
            pltpu.VMEM((2 * rows, BLOCK, features), BF16),
            pltpu.VMEM((2 * rows, HEAD_DIM, HEAD_DIM), BF16),
            pltpu.VMEM((cols, tokens, features), BF16),
            pltpu.VMEM((tokens, features), BF16),
            pltpu.VMEM((QBLOCKS, HEADS_DEV, BLOCK, TILES * BLOCK), F32),
            pltpu.VMEM((tokens, features), F32),
            *reducing,
            *reducing,
            dma((3, 2, chips // 2, 2)),
            dma((3, 2, chips // 2, 2)),
            dma((3, chips)),
            dma((3, chips)),
            dma((2, ycount // 2, 2)),
            dma((2, ycount // 2, 2)),
            dma((2, 2, chips // 2, 2)),
            dma((2, 2, chips // 2, 2)),
            dma((4,)),
            dma((4,)),
        ],
        compiler_params=pltpu.CompilerParams(
            collective_id=0, has_side_effects=True, vmem_limit_bytes=40 * 2**20
        ),
        cost_estimate=pl.CostEstimate(
            flops=flops, bytes_accessed=16 * tokens * features, transcendentals=0
        ),
        name="relay",
    )(
        random_table.reshape(-1),
        grad_output,
        queries[0],
        keys[0],
        values[0],
        value_weight[0],
    )
    return tuple(array[None] for array in grads)


def solution(mesh):
    in_specs = (
        P("row", "col"),
        P("pipe", "row", "col"),
        P("pipe", "row", "col"),
        P("pipe", "row", "col"),
        P("pipe", "col", "row"),
        P("pipe", None, "col", None),
    )
    out_specs = (P("pipe", "row", "col"), P("pipe", "row", "col"), P("pipe", "row", "col"))
    return jax.shard_map(body, mesh=mesh, in_specs=in_specs, out_specs=out_specs, check_vma=False)
```

time: 463 us -> 193 us (0.42)
  the two profiles are of different devices: /device:TPU:2 before, /device:TPU:8 now
where the time goes in v1:
time: 193 us
  Pallas kernels  186 us (96%)
  local copies, waits for them, and re-layouts  5.95 us (3%)
    pallas_call x1, Pallas kernels, body(): pl.pallas_call(run, out_shape=(out, out, out), in_specs=[pl.BlockSpec(mem...  186 us
    unnamed x16, local copies, waits for them, and re-layouts  5.73 us

profile of v1, /device:TPU:8, one launch (start us, length us, event | category | flops | bytes accessed | tf_op | source)
XLA Modules:
  0.0 192.9 jit_solution(15326429903354771867)
XLA Ops:
  0.6 0.0 copy-start.5
  0.6 0.7 copy-done.5
  1.3 0.0 copy-start
  1.3 0.0 copy-start.1
  1.3 0.1 copy.9
  1.4 0.2 reshape.9.refs_0_
  1.7 0.5 copy-done
  2.2 0.0 copy-done.1
  2.2 0.0 copy-start.2
  2.2 0.8 copy-done.2
  3.0 0.0 copy-start.3
  3.0 0.8 copy-done.3
  3.9 0.0 copy-start.4
  3.9 0.8 copy-done.4
  4.7 186.3 %relay.1 = (bf16[128,256]{1,0:T(8,128)(2,1)S(1)}, bf16[128,256]{1,0:T(8,128)(2,1)S(1)}, bf16[128,256]{1,0:T(8,128)(2,1)S(1)}) custom-call(s32[384]{0:T(512)S(1)} %reshape.9.refs_0_, bf16[128,256]{1,0:T(8,128)(2,1)S(1)} %copy-done, bf16[128,256]{1,0:T(8,128)(2,1)S(1)} %bitcast.10, bf16[128,256]{1,0:T(8,128)(2,1)S(1)} %bitcast.11, ...), custom_call_target="tpu_custom_call" | custom-call | flops 520093696 | bytes 524288 | tf_op jit(solution)/shard_map/relay/pallas_call | solution.py:479
  191.0 0.6 copy.13
  191.7 0.6 copy.14
  192.3 0.6 copy.15
Async XLA Ops:
  0.6 0.7 copy-start.5
  1.3 0.8 copy-start
  1.3 0.9 copy-start.1
  2.2 0.8 copy-start.2
  3.0 0.8 copy-start.3
  3.9 0.8 copy-start.4

commit v2 on v1

--- a/solution.py
+++ b/solution.py
@@ -28,6 +28,24 @@
                 streams.remove(stream)
 
 
+def take(stream, delay, count):
+    for _ in range(delay):
+        yield
+    for _ in range(count):
+        if next(stream, "end") == "end":
+            return
+        yield
+
+
+def tree(half, skip):
+    if not skip:
+        return [(i, i + 1) for i in range(half)]
+    edges = []
+    for i in range(0, half, 2):
+        edges += [(i, j) for j in (i + 2, i + 1) if j <= half]
+    return edges
+
+
 def lanes(head):
     return pl.ds(head * HEAD_DIM, HEAD_DIM)
 
@@ -37,7 +55,7 @@
     cols,
     table,
     grad,
-    query,
+    query_hbm,
     key,
     value,
     weight,
@@ -48,6 +66,7 @@
     value_all,
     weight_all,
     grad_all,
+    query,
     up,
     probs,
     acc,
@@ -71,6 +90,7 @@
     sum_recv,
     one_send,
     one_recv,
+    load_sem,
 ):
     chips = rows // 2
     ycount = cols // 2
@@ -81,16 +101,41 @@
     chip, core = row // 2, lax.rem(row, 2)
     ypos, xpos = col // 2, lax.rem(col, 2)
     sibling = row + 1 - 2 * core
-    row_next = ({"row": lax.rem(row + 2, rows)}, {"row": lax.rem(row + rows - 2, rows)})
-    col_next = ({"col": lax.rem(col + 2, cols)}, {"col": lax.rem(col + cols - 2, cols)})
+
+    def chip_at(hops):
+        return {"row": lax.rem(row + 2 * hops + rows, rows)}
+
+    def place_at(hops):
+        return {"col": lax.rem(col + 2 * hops + cols, cols)}
+
     to_sibling = {"row": sibling}
     to_partner = {"col": col + 1 - 2 * xpos}
     to_pipe = {"pipe": 1 - pipe}
 
+    own_key = [
+        pltpu.make_async_copy(key.at[i], key_all.at[2 * row + i], load_sem.at[i]) for i in range(2)
+    ]
+    loads = [
+        pltpu.make_async_copy(weight.at[i], weight_all.at[2 * row + i], load_sem.at[2 + i])
+        for i in range(2)
+    ]
+    loads += [
+        pltpu.make_async_copy(value.at[i], value_all.at[2 * row + i], load_sem.at[4 + i])
+        for i in range(2)
+    ]
+    loads.append(pltpu.make_async_copy(query_hbm, query, load_sem.at[6]))
+    own_grad = pltpu.make_async_copy(grad, up, load_sem.at[7])
+    for load in own_key + loads:
+        load.start()
+
     barrier = pltpu.get_barrier_semaphore()
-    for device in (*row_next, *col_next, to_sibling, to_partner, to_pipe):
+    greeted = [chip_at(hops) for hops in (1, -1, 2, -2)]
+    greeted += [place_at(1), place_at(-1), to_sibling, to_partner, to_pipe]
+    for device in greeted:
         pl.semaphore_signal(barrier, inc=1, device_id=device, device_id_type=MESH)
-    pl.semaphore_wait(barrier, 7)
+    for load in own_key:
+        load.wait()
+    pl.semaphore_wait(barrier, len(greeted))
 
     def remote(src, dst, send, recv, device):
         return pltpu.make_async_remote_copy(
@@ -102,73 +147,56 @@
             device_id_type=MESH,
         )
 
-    def gather(sent, buf, pos, size, entry, devices, send, recv, shared=None, second=None, arrive=None):
+    def gather(sent, buf, pos, size, entry, device_at, skip, send, recv, shared=None, second=None, arrive=None):
         half = size // 2
+        edges = tree(half, skip)
 
         def ref(offset, item):
             return buf.at[entry(lax.rem(pos + offset + size, size), item)]
 
-        def copy(way, step, item):
-            offset = step if way else -step
+        def copy(way, start, end, item, offset):
+            block = ref(offset, item)
             return remote(
-                ref(offset, item),
-                ref(offset, item),
-                send.at[way, step, item],
-                recv.at[way, step, item],
-                devices[way],
+                block,
+                block,
+                send.at[way, end - 1, item],
+                recv.at[way, end - 1, item],
+                device_at(start - end if way else end - start),
             )
 
-        def push(way, step, item):
-            if step < half - 1 or (step == half - 1 and way == item):
-                made = copy(way, step, item)
-                made.start()
-                sent.append(made)
-
-        def arrived(way, step, item):
-            offset = step if way else -step
-            remote(
-                ref(offset, item),
-                ref(offset, item),
-                send.at[way, step - 1, item],
-                recv.at[way, step - 1, item],
-                devices[way],
-            ).wait_recv()
-
-        def share(offset):
-            if shared is not None:
-                shared(offset)
+        def push(way, distance, item):
+            for start, end in edges:
+                if start == distance and (end < half or way == item):
+                    made = copy(way, start, end, item, distance if way else -distance)
+                    made.start()
+                    sent.append(made)
 
         for item in range(2):
             if item == 1 and second is not None:
                 second()
             for way in range(2):
                 push(way, 0, item)
-        share(0)
+        if shared is not None:
+            shared(0)
         if arrive is not None:
             arrive(0, 0)
             arrive(0, 1)
         yield
-        for step in range(1, half):
+        for start, end in edges:
             for item in range(2):
-                for way in range(2):
-                    arrived(way, step, item)
-                    push(way, step, item)
-                if item == 1:
-                    share(-step)
-                    share(step)
+                ways = [way for way in range(2) if end < half or way == item]
+                for way in ways:
+                    copy(way, start, end, item, end if way else -end).wait_recv()
+                    push(way, end, item)
+                if shared is not None and item == 1:
+                    for offset in (-end, end)[: 2 if end < half else 1]:
+                        shared(offset)
                 if arrive is not None:
-                    arrive(-step, item)
-                    arrive(step, item)
+                    for way in ways:
+                        arrive(end if way else -end, item)
                 yield
-        for way in range(2):
-            arrived(way, half, way)
-        share(half)
-        if arrive is not None:
-            arrive(half, 0)
-            arrive(half, 1)
-        yield
-
-    def row_gather(sent, which, buf):
+
+    def row_gather(sent, which, buf, skip=True):
         shares = []
 
         def entry(place, item):
@@ -190,7 +218,8 @@
             chip,
             chips,
             entry,
-            row_next,
+            chip_at,
+            skip,
             ring_send.at[which],
             ring_recv.at[which],
             shared=shared,
@@ -290,7 +319,10 @@
     def reduce(sent, which, own, sib, local, sbuf, rbuf, result):
         half = chips // 2
 
-        def contribution(offset, part, head):
+        def contribution(offset, part):
+            return jnp.concatenate([tile(offset, part, head) for head in range(HEADS_DEV)], axis=1)
+
+        def tile(offset, part, head):
             place = lax.rem(chip + offset + chips, chips)
             block = 4 * place + 2 * core + part
             found = own[head * SLOTS + find(row, block, head)].astype(F32)
@@ -308,44 +340,45 @@
                 found += sib[head * SLOTS + rim].astype(F32)
             return found
 
-        def copy(way, step, part):
+        edges = tree(half, True)
+
+        def copy(way, start, end, part):
             return remote(
-                sbuf.at[way, step, part],
-                rbuf.at[way, step, part],
-                sum_send.at[which, way, step, part],
-                sum_recv.at[which, way, step, part],
-                row_next[way],
+                sbuf.at[way, end - 1, part],
+                rbuf.at[way, end - 1, part],
+                sum_send.at[which, way, end - 1, part],
+                sum_recv.at[which, way, end - 1, part],
+                chip_at(start - end if way else end - start),
             )
+
+        def arrived(way, distance, part):
+            for start, end in edges:
+                if start == distance and (end < half or way == part):
+                    copy(way, start, end, part).wait_recv()
+                    yield rbuf[way, end - 1, part].astype(F32)
 
         exchange = remote(own, sib, one_send.at[which], one_recv.at[which], to_sibling)
         exchange.start()
         exchange.wait_recv()
         sent.append(exchange)
-        for step in range(half):
+        for start, end in sorted(edges, key=lambda edge: (-edge[0], edge[1] % 2 == 0, -edge[1])):
             for part in range(2):
                 for way in range(2):
-                    if step == 0 and part != way:
+                    if end == half and part != way:
                         continue
-                    distance = half - step
-                    offset = -distance if way else distance
-                    terms = [contribution(offset, part, head) for head in range(HEADS_DEV)]
-                    if step > 1 or (step == 1 and part == way):
-                        copy(way, step - 1, part).wait_recv()
-                        for head in range(HEADS_DEV):
-                            terms[head] += rbuf[way, step - 1, part, :, lanes(head)].astype(F32)
-                    for head in range(HEADS_DEV):
-                        sbuf[way, step, part, :, lanes(head)] = terms[head].astype(BF16)
-                    made = copy(way, step, part)
+                    total = contribution(-end if way else end, part)
+                    for term in arrived(way, end, part):
+                        total += term
+                    sbuf[way, end - 1, part] = total.astype(BF16)
+                    made = copy(way, start, end, part)
                     made.start()
                     sent.append(made)
                 yield
         for part in range(2):
-            total = local[part] + jnp.concatenate(
-                [contribution(0, part, head) for head in range(HEADS_DEV)], axis=1
-            )
+            total = local[part] + contribution(0, part)
             for way in range(2):
-                copy(way, half - 1, part).wait_recv()
-                total += rbuf[way, half - 1, part].astype(F32)
+                for term in arrived(way, 0, part):
+                    total += term
             result(part, total.astype(BF16))
         yield
 
@@ -390,7 +423,8 @@
             ypos,
             ycount,
             col_entry,
-            col_next,
+            place_at,
+            False,
             col_send,
             col_recv,
             second=lambda: exchange().wait_recv(),
@@ -406,21 +440,20 @@
     def value_reduce(sent):
         yield from reduce(sent, 0, v_own, v_sib, v_local, v_send, v_recv, keep_value_grad)
 
-    own_rows = pl.ds(2 * row, 2)
-    key_all[own_rows] = key[...].reshape(2, BLOCK, key.shape[1])
-    value_all[own_rows] = value[...].reshape(2, BLOCK, value.shape[1])
-    weight_all[own_rows] = weight[...].reshape(2, HEAD_DIM, HEAD_DIM)
-
     @pl.when(pipe == 1)
     def _():
         sent = []
+        own_grad.start()
         drive(row_gather(sent, 0, key_all))
+        for load in loads:
+            load.wait()
+        own_grad.wait()
         make_probs()
-        up[...] = grad[...]
         value_terms()
-        drive(value_reduce(sent))
+        weights = row_gather(sent, 1, weight_all)
+        drive(value_reduce(sent), take(weights, 10, 4))
         acc[...] = up[...].astype(F32)
-        drive(col_gather(sent, False), row_gather(sent, 1, weight_all))
+        drive(col_gather(sent, False), weights)
 
         def step(place, carry):
             project(place)
@@ -441,9 +474,10 @@
     def _():
         sent = []
         drive(row_gather(sent, 0, key_all))
+        for load in loads:
+            load.wait()
         make_probs()
-        drive(row_gather(sent, 1, weight_all))
-        drive(row_gather(sent, 2, value_all))
+        drive(row_gather(sent, 1, weight_all), row_gather(sent, 2, value_all))
         upstream_copy().wait_recv()
         value_terms()
         drive(value_reduce(sent), key_terms())
@@ -479,13 +513,14 @@
     grads = pl.pallas_call(
         run,
         out_shape=(out, out, out),
-        in_specs=[pl.BlockSpec(memory_space=pltpu.SMEM)] + [vmem] * 5,
+        in_specs=[pl.BlockSpec(memory_space=pltpu.SMEM)] + [pl.BlockSpec(memory_space=pl.ANY)] * 5,
         out_specs=(vmem, vmem, vmem),
         scratch_shapes=[
             pltpu.VMEM((2 * rows, BLOCK, features), BF16),
             pltpu.VMEM((2 * rows, BLOCK, features), BF16),
             pltpu.VMEM((2 * rows, HEAD_DIM, HEAD_DIM), BF16),
             pltpu.VMEM((cols, tokens, features), BF16),
+            pltpu.VMEM((tokens, features), BF16),
             pltpu.VMEM((tokens, features), BF16),
             pltpu.VMEM((QBLOCKS, HEADS_DEV, BLOCK, TILES * BLOCK), F32),
             pltpu.VMEM((tokens, features), F32),
@@ -501,9 +536,10 @@
             dma((2, 2, chips // 2, 2)),
             dma((4,)),
             dma((4,)),
+            dma((8,)),
         ],
         compiler_params=pltpu.CompilerParams(
-            collective_id=0, has_side_effects=True, vmem_limit_bytes=40 * 2**20
+            collective_id=0, has_side_effects=True, vmem_limit_bytes=56 * 2**20
         ),
         cost_estimate=pl.CostEstimate(
             flops=flops, bytes_accessed=16 * tokens * features, transcendentals=0
@@ -513,9 +549,9 @@
         random_table.reshape(-1),
         grad_output,
         queries[0],
-        keys[0],
-        values[0],
-        value_weight[0],
+        keys.reshape(2, BLOCK, features),
+        values.reshape(2, BLOCK, features),
+        value_weight.reshape(2, HEAD_DIM, HEAD_DIM),
     )
     return tuple(array[None] for array in grads)
 

time: 193 us -> 158 us (0.82)
  Pallas kernels: 186 us -> 152 us
    pallas_call x1, Pallas kernels: 186 us -> 152 us  [body(): pl.pallas_call(run, out_shape=(out, out, out), in_specs=[pl.BlockSpec(mem...]
    unnamed x16 -> x10, local copies, waits for them, and re-layouts: 5.73 us -> 3.79 us
where the time goes in v2:
time: 158 us; the launch traced here: 157 us
  Pallas kernels  152 us (96%)
  local copies, waits for them, and re-layouts  4.59 us (3%)
    pallas_call x1, Pallas kernels, body(): pl.pallas_call(run, out_shape=(out, out, out), in_specs=[pl.BlockSpec(mem...  152 us
    unnamed x10, local copies, waits for them, and re-layouts  3.79 us

profile of v2, /device:TPU:8, one launch (start us, length us, event | category | flops | bytes accessed | tf_op | source)
XLA Modules:
  0.0 157.4 jit_solution(4929290084881140433)
XLA Ops:
  0.6 0.0 copy-start.2
  0.6 0.7 copy-done.2
  1.3 0.1 copy.9
  1.4 0.8 reshape.18.refs_0_
  2.2 152.2 %relay.1 = (bf16[128,256]{1,0:T(8,128)(2,1)}, bf16[128,256]{1,0:T(8,128)(2,1)}, bf16[128,256]{1,0:T(8,128)(2,1)}) custom-call(s32[384]{0:T(512)} %reshape.18.refs_0_, bf16[128,256]{1,0:T(8,128)(2,1)} %refs_1_.1, bf16[128,256]{1,0:T(8,128)(2,1)} %bitcast.10, bf16[2,64,256]{2,1,0:T(8,128)(2,1)} %bitcast.11, bf16[2,64,256]{2,1,0:T(8,128)(2,1)} %bitcast.12, ...), custom_call_target="tpu_custom_call" | custom-call | flops 520093696 | bytes 524288 | tf_op jit(solution)/shard_map/relay/pallas_call | solution.py:513
  154.4 0.0 copy-start.1
  154.4 1.5 copy.13
  155.9 0.0 copy-done.1
  155.9 0.0 copy-start
  155.9 0.6 copy.14
  156.6 0.2 copy-done
  156.8 0.6 copy.15
Async XLA Ops:
  0.6 0.7 copy-start.2
  154.4 1.5 copy-start.1
  155.9 0.9 copy-start

commit v3 on v2

v3 whole, which is shorter than its diff:
```python
import math

import jax
import jax.numpy as jnp
from jax import lax
from jax.experimental import pallas as pl
from jax.experimental.pallas import tpu as pltpu
from jax.sharding import PartitionSpec as P

HEAD_DIM = 128
BLOCK = 64
RANDOMS = 3
QBLOCKS = 2
TILES = 3 + RANDOMS
ENTRIES = QBLOCKS * RANDOMS
ZERO, RIM_LEFT, RIM_RIGHT, SLOTS = ENTRIES, ENTRIES + 1, ENTRIES + 2, ENTRIES + 3
MESH = pl.DeviceIdType.MESH
BF16 = jnp.bfloat16
F32 = jnp.float32


def drive(*streams):
    streams = list(streams)
    while streams:
        for stream in list(streams):
            if next(stream, "end") == "end":
                streams.remove(stream)


def take(stream, delay, count):
    for _ in range(delay):
        yield
    for _ in range(count):
        if next(stream, "end") == "end":
            return
        yield


def tree(half, skip):
    if not skip:
        return [(i, i + 1) for i in range(half)]
    edges = []
    for i in range(0, half, 2):
        edges += [(i, j) for j in (i + 2, i + 1) if j <= half]
    return edges


def chain(*streams):
    for stream in streams:
        yield from stream


def lanes(head):
    return pl.ds(pl.multiple_of(head * HEAD_DIM, HEAD_DIM), HEAD_DIM)


def kernel(
    rows,
    cols,
    table_hbm,
    grad_hbm,
    query_hbm,
    key_hbm,
    value_hbm,
    weight_hbm,
    input_out,
    query_out,
    key_out,
    table_own,
    table_other,
    key_zero,
    key_one,
    value_zero,
    value_one,
    weight_all,
    grad_all,
    query,
    up,
    probs,
    acc,
    own_zero,
    own_one,
    own_two,
    own_three,
    sib_zero,
    sib_one,
    sib_two,
    sib_three,
    terms_local,
    sum_out,
    sum_in,
    part_out,
    part_in,
    last_in,
    results,
    stage,
    ring_send,
    ring_recv,
    sib_send,
    sib_recv,
    weight_send,
    weight_recv,
    share_send,
    share_recv,
    col_send,
    col_recv,
    sum_send,
    sum_recv,
    swap_send,
    swap_recv,
    part_send,
    part_recv,
    load_sem,
):
    chips = rows // 2
    ycount = cols // 2
    scale = 1.0 / math.sqrt(HEAD_DIM)
    key_all, value_all = (key_zero, key_one), (value_zero, value_one)
    terms_own = (own_zero, own_one, own_two, own_three)
    terms_sib = (sib_zero, sib_one, sib_two, sib_three)
    pipe = lax.axis_index("pipe")
    row = lax.axis_index("row")
    col = lax.axis_index("col")
    chip, core = row // 2, lax.rem(row, 2)
    ypos, xpos = col // 2, lax.rem(col, 2)
    sibling = row + 1 - 2 * core
    other_col = col + 1 - 2 * xpos
    to_sibling = {"row": sibling}
    to_pipe = {"pipe": 1 - pipe}
    quad = [(pipe, xpos), (1 - pipe, xpos), (pipe, 1 - xpos), (1 - pipe, 1 - xpos)]
    to_quad = [{"pipe": p, "col": 2 * ypos + x} for p, x in quad]

    def chip_at(hops):
        return {"row": lax.rem(row + 2 * hops + rows, rows)}

    def place_at(hops):
        return {"col": lax.rem(col + 2 * hops + cols, cols)}

    def remote(src, dst, send, recv, device):
        return pltpu.make_async_remote_copy(
            src_ref=src,
            dst_ref=dst,
            send_sem=send,
            recv_sem=recv,
            device_id=device,
            device_id_type=MESH,
        )

    def load(src, dst, slot):
        return pltpu.make_async_copy(src, dst, load_sem.at[slot])

    mine, other = lanes(pipe), lanes(1 - pipe)
    loads = [load(query_hbm.at[:, mine], query.at[pipe], 2)]
    loads.append(load(grad_hbm.at[:, mine], up.at[1], 3))
    loads.append(load(table_hbm, table_own, 4))

    def own_load(kind, section, i):
        src, dst = ((key_hbm, key_all), (value_hbm, value_all))[kind]
        slot = (0, 5)[kind] + i
        return load(src.at[i, :, mine], dst[section].at[2 * row + i], slot)

    def swap(kind, section, i):
        src, dst = ((key_hbm, key_all), (value_hbm, value_all))[kind]
        slot = (0, 4)[kind] + i
        return remote(
            src.at[i, :, other],
            dst[section].at[2 * row + i],
            swap_send.at[slot],
            swap_recv.at[slot],
            to_pipe,
        )

    def here_or_there(here, there):
        for section in range(2):
            if here is not None:
                pl.when(pipe == section)(lambda section=section: here(section))
            if there is not None:
                pl.when(pipe != section)(lambda section=section: there(section))

    def start_loads(section):
        for kind in range(2):
            for i in range(2):
                own_load(kind, section, i).start()

    def start_swaps(kind):
        def start(section):
            for i in range(2):
                swap(kind, section, i).start()

        here_or_there(start, None)

    def settle(kind):
        def here(section):
            for i in range(2):
                own_load(kind, section, i).wait()

        def there(section):
            for i in range(2):
                swap(kind, section, i).wait_recv()

        here_or_there(here, there)

    here_or_there(start_loads, None)
    for made in loads:
        made.start()

    barrier = pltpu.get_barrier_semaphore()
    greeted = [chip_at(hops) for hops in (1, -1, 2, -2)]
    greeted += [place_at(hops) for hops in ((1, -1, 2, -2) if ycount > 2 else (1, -1))]
    greeted += to_quad[1:]
    greeted += [{**device, "row": sibling} for device in to_quad]
    for device in greeted:
        pl.semaphore_signal(barrier, inc=1, device_id=device, device_id_type=MESH)
    pl.semaphore_wait(barrier, len(greeted))

    swaps = [
        remote(
            query_hbm.at[:, other], query.at[pipe], swap_send.at[2], swap_recv.at[2], to_pipe
        ),
        remote(table_hbm, table_other, swap_send.at[3], swap_recv.at[3], to_pipe),
    ]
    start_swaps(0)
    for made in swaps:
        made.start()
    start_swaps(1)
    sent = list(swaps)

    keep = (pipe == core) & (xpos == lax.rem(chip, 2))

    def weight_block():
        return weight_all.at[pipe, chip // 2, pl.ds(2 * xpos, 2)]

    def weight_move():
        return remote(
            weight_hbm,
            weight_block(),
            swap_send.at[6],
            weight_recv.at[0, chips // 2, xpos],
            {"pipe": core, "row": 2 * chip + pipe, "col": 2 * ypos + lax.rem(chip, 2)},
        )

    @pl.when(keep)
    def _():
        pltpu.make_async_copy(
            weight_hbm, weight_block(), weight_recv.at[0, chips // 2, xpos]
        ).start()

    @pl.when(jnp.logical_not(keep))
    def _():
        weight_move().start()

    def gather(buf, pos, size, entry, device_at, skip, send, recv, shared=None, arrive=None):
        half = size // 2
        edges = tree(half, skip)

        def ref(offset, item):
            return buf.at[entry(lax.rem(pos + offset + size, size), item)]

        def copy(way, start, end, item, offset):
            block = ref(offset, item)
            return remote(
                block,
                block,
                send.at[way, end - 1, item],
                recv.at[way, end - 1, item],
                device_at(start - end if way else end - start),
            )

        def push(way, distance, item):
            for start, end in edges:
                if start == distance and (end < half or way == item):
                    made = copy(way, start, end, item, distance if way else -distance)
                    made.start()
                    sent.append(made)

        for item in range(2):
            for way in range(2):
                push(way, 0, item)
        if shared is not None:
            shared(0)
        if arrive is not None:
            arrive(0, 0)
            arrive(0, 1)
        yield
        for start, end in edges:
            for item in range(2):
                ways = [way for way in range(2) if end < half or way == item]
                for way in ways:
                    copy(way, start, end, item, end if way else -end).wait_recv()
                    push(way, end, item)
                if shared is not None and item == 1:
                    for offset in (-end, end)[: 2 if end < half else 1]:
                        shared(offset)
                if arrive is not None:
                    for way in ways:
                        arrive(end if way else -end, item)
                yield

    def row_gather(which, buf, skip=True):
        shares = []

        def entry(place, item):
            return 4 * place + 2 * core + item

        def shared(offset):
            place = lax.rem(chip + offset + chips, chips)
            block = buf.at[pl.ds(4 * place + 2 * core, 2)]
            slot = (offset + chips) % chips
            made = remote(
                block, block, sib_send.at[which, slot], sib_recv.at[which, slot], to_sibling
            )
            made.start()
            shares.append(made)

        yield from gather(
            buf,
            chip,
            chips,
            entry,
            chip_at,
            skip,
            ring_send.at[which],
            ring_recv.at[which],
            shared=shared,
        )
        for made in shares:
            made.wait_recv()
        sent.extend(shares)

    def weight_gather():
        half = chips // 2
        edges = tree(half, True)
        holds = lax.rem(chip, 2) == xpos

        def place(offset):
            return lax.rem(chip + offset + chips, chips) // 2

        def copy(way, start, end, item, offset):
            block = weight_all.at[core, place(offset), pl.ds(2 * item, 2)]
            return remote(
                block,
                block,
                weight_send.at[way, end - 1, item],
                weight_recv.at[way, end - 1, item],
                chip_at(start - end if way else end - start),
            )

        def pushes(way, distance, item):
            for start, end in edges:
                if start == distance and (end < half or way == item):
                    yield copy(way, start, end, item, distance if way else -distance)

        def share(spot):
            block = weight_all.at[core, spot]
            return remote(
                block, block, share_send.at[spot], share_recv.at[spot], to_sibling
            )

        def opening():
            for item in range(2):
                block = weight_all.at[core, chip // 2, pl.ds(2 * item, 2)]
                pltpu.make_async_copy(block, block, weight_recv.at[0, half, item]).wait()
            for item in range(2):
                for way in range(2):
                    for made in pushes(way, 0, item):
                        made.start()
            share(chip // 2).start()

        pl.when(holds)(opening)
        yield
        for start, end in edges:
            for item in range(2):

                def step(start=start, end=end, item=item):
                    for way in range(2):
                        if end == half and way != item:
                            continue
                        copy(way, start, end, item, end if way else -end).wait_recv()
                        for made in pushes(way, end, item):
                            made.start()
                    if item == 1:
                        for offset in (-end, end)[: 2 if end < half else 1]:
                            share(place(offset)).start()

                pl.when(holds if end % 2 == 0 else jnp.logical_not(holds))(step)
                yield

        for spot in range(half):
            share(spot).wait_recv()

        def ending():
            for distance in range(0, half, 2):
                for item in range(2):
                    for way in range(2):
                        for made in pushes(way, distance, item):
                            made.wait_send()

        def finish():
            pl.when(holds)(ending)
            for spot in range(half):
                share(spot).wait_send()

        finishing.append(finish)

    finishing = []

    def named(section, owner):
        found = []
        for n in range(QBLOCKS):
            for t in range(RANDOMS):
                at = owner * 12 + n * 6 + pipe * 3 + t
                found.append(jnp.where(pipe == section, table_own[at], table_other[at]))
        return found

    def tiles(buf, section, n):
        block = 2 * row + n
        ids = [
            lax.rem(block + 2 * rows - 1, 2 * rows),
            block,
            lax.rem(block + 1, 2 * rows),
            *named(section, row)[n * RANDOMS : (n + 1) * RANDOMS],
        ]
        return jnp.concatenate([buf[section][i] for i in ids], axis=0)

    def rows_of(ref, section, n):
        return ref[section, pl.ds(n * BLOCK, BLOCK)]

    def make_probs(section):
        for n in range(QBLOCKS):
            scores = scale * lax.dot_general(
                rows_of(query, section, n),
                tiles(key_all, section, n),
                (((1,), (1,)), ((), ())),
                preferred_element_type=F32,
            )
            place = lax.broadcasted_iota(jnp.int32, scores.shape, 1) // BLOCK
            block = 2 * row + n
            gone_left = jnp.where(block == 0, 0, -1)
            gone_right = jnp.where(block == 2 * rows - 1, 2, -1)
            scores = jnp.where((place == gone_left) | (place == gone_right), -1e30, scores)
            top = jnp.max(scores, axis=1, keepdims=True)
            total = jnp.sum(jnp.exp(scores - top), axis=1, keepdims=True)
            probs[section, n] = jnp.exp(scores - (top + jnp.log(total)))

    def keep_terms(which, n, terms):
        terms = terms.astype(BF16)
        part = [terms[t * BLOCK : (t + 1) * BLOCK] for t in range(TILES)]
        for t in range(RANDOMS):
            terms_own[which][n * RANDOMS + t] = part[3 + t]
        if n == 0:
            terms_own[which][ZERO] = jnp.zeros_like(part[0])
            terms_own[which][RIM_LEFT] = part[0]
            terms_local[which, 0] = part[1].astype(F32)
            terms_local[which, 1] = part[2].astype(F32)
        else:
            terms_local[which, 0] += part[0].astype(F32)
            terms_local[which, 1] += part[1].astype(F32)
            terms_own[which][RIM_RIGHT] = part[2]

    def transposed_dot(left, right):
        return lax.dot_general(left, right, (((0,), (0,)), ((), ())), preferred_element_type=F32)

    def value_terms(section):
        for n in range(QBLOCKS):
            low = probs[section, n].astype(BF16)
            keep_terms(section, n, transposed_dot(low, rows_of(up, section, n)))

    def key_terms(section):
        for n in range(QBLOCKS):
            prob = probs[section, n]
            dprobs = lax.dot_general(
                rows_of(up, section, n),
                tiles(value_all, section, n),
                (((1,), (1,)), ((), ())),
                preferred_element_type=F32,
            )
            low = prob.astype(BF16).astype(F32)
            delta = jnp.sum(low * dprobs, axis=1, keepdims=True)
            dscores = (prob * (dprobs - delta) * scale).astype(BF16)
            results[section, 1, pl.ds(n * BLOCK, BLOCK)] = jnp.dot(
                dscores, tiles(key_all, section, n), preferred_element_type=F32
            ).astype(BF16)
            keep_terms(2 + section, n, transposed_dot(dscores, rows_of(query, section, n)))
            yield
        deliver(section, 1)
        yield

    outs = (input_out, query_out, key_out)

    def delivery(section, kind):
        return remote(
            results.at[section, kind],
            stage.at[kind],
            swap_send.at[7 + kind],
            swap_recv.at[7 + kind],
            to_pipe,
        )

    def deliver(section, kind):
        @pl.when(pipe == section)
        def _():
            outs[kind][:, mine] = results[section, kind]

        @pl.when(pipe != section)
        def _():
            delivery(section, kind).start()

    def reduce(section, which, result):
        half = chips // 2
        edges = tree(half, True)
        own_names, sib_names = named(section, row), named(section, sibling)

        def find(names, block):
            found = ZERO
            for slot, name in enumerate(names):
                found = jnp.where(name == block, slot, found)
            return found

        def contribution(offset, part):
            place = lax.rem(chip + offset + chips, chips)
            block = 4 * place + 2 * core + part
            total = terms_own[which][find(own_names, block)].astype(F32)
            total += terms_sib[which][find(sib_names, block)].astype(F32)
            rim = None
            if (offset, part) == (0, 0):
                rim = jnp.where(core == 1, RIM_RIGHT, ZERO)
            if (offset, part) == (0, 1):
                rim = jnp.where(core == 0, RIM_LEFT, ZERO)
            if (offset, part) == (1, 0):
                rim = jnp.where(core == 0, RIM_RIGHT, ZERO)
            if (offset, part) == (-1, 1):
                rim = jnp.where(core == 1, RIM_LEFT, ZERO)
            if rim is not None:
                total += terms_sib[which][rim].astype(F32)
            return total

        def copy(way, start, end, part):
            return remote(
                sum_out.at[which, way, end - 1, part],
                sum_in.at[which, way, end - 1, part],
                sum_send.at[which, way, end - 1, part],
                sum_recv.at[which, way, end - 1, part],
                chip_at(start - end if way else end - start),
            )

        def arrived(way, distance, part):
            for start, end in edges:
                if start == distance and (end < half or way == part):
                    copy(way, start, end, part).wait_recv()
                    yield sum_in[which, way, end - 1, part].astype(F32)

        exchange = remote(
            terms_own[which],
            terms_sib[which],
            swap_send.at[10 + which],
            swap_recv.at[10 + which],
            to_sibling,
        )
        exchange.start()
        exchange.wait_recv()
        sent.append(exchange)
        order = sorted(edges, key=lambda edge: (-edge[0], edge[1] % 2 == 0, -edge[1]))
        for start, end in order:
            for part in range(2):
                for way in range(2):
                    if end == half and part != way:
                        continue
                    total = contribution(-end if way else end, part)
                    for term in arrived(way, end, part):
                        total += term
                    sum_out[which, way, end - 1, part] = total.astype(BF16)
                    made = copy(way, start, end, part)
                    made.start()
                    sent.append(made)
                yield
        for part in range(2):
            total = terms_local[which, part] + contribution(0, part)
            for way in range(2):
                for term in arrived(way, 0, part):
                    total += term
            result(part, total.astype(BF16))
        yield

    def value_reduce(section):
        def keep_part(part, total):
            grad_all[section, 2 * ypos + part] = total

        yield from reduce(section, section, keep_part)

    def key_reduce(section):
        def keep_part(part, total):
            results[section, 2, pl.ds(part * BLOCK, BLOCK)] = total

        yield from reduce(section, 2 + section, keep_part)
        deliver(section, 2)

    def col_gather(section):
        acc[...] = jnp.zeros_like(acc)

        def arrive(offset, item):
            place = lax.rem(ypos + offset + ycount, ycount)
            acc[pl.ds(item * BLOCK, BLOCK)] += lax.dot_general(
                grad_all[section, 2 * place + item],
                weight_all[section, place].reshape(4 * HEAD_DIM, HEAD_DIM),
                (((1,), (1,)), ((), ())),
                preferred_element_type=F32,
            )

        yield from gather(
            grad_all.at[section],
            ypos,
            ycount,
            lambda place, item: 2 * place + item,
            place_at,
            True,
            col_send.at[section],
            col_recv.at[section],
            arrive=arrive,
        )

    def own_share():
        return acc[:, lanes(2 * xpos + pipe)]

    def spread_partials():
        for head in range(4):
            part_out[1, head] = acc[:, lanes(head)].astype(BF16)
        copies = [
            remote(
                part_out.at[1, 2 * x + p],
                part_in.at[j],
                part_send.at[1, j],
                part_recv.at[1, j],
                to_quad[j],
            )
            for j, (p, x) in enumerate(quad)
            if j
        ]
        for made in copies:
            made.start()
        sent.extend(copies)
        return copies

    def last_copy(j):
        x = quad[j][1]
        return remote(
            part_out.at[0, pl.ds(2 * x, 2)],
            last_in.at[j],
            part_send.at[0, j],
            part_recv.at[0, j],
            {"pipe": 0, "col": 2 * ypos + x},
        )

    def last_projection():
        yield from col_gather(0)
        acc[:, lanes(2 * xpos + pipe)] += up[0].astype(F32)
        for head in range(4):
            part_out[0, head] = acc[:, lanes(head)].astype(BF16)

        @pl.when(pipe == 1)
        def _():
            for j in (1, 3):
                last_copy(j).start()

        @pl.when(pipe == 0)
        def _():
            last_copy(2).start()

        yield

    settle(0)
    weights = weight_gather()
    drive(row_gather(0, key_all[1]), take(weights, 4, 8))
    for made in loads:
        made.wait()
    for made in swaps:
        made.wait_recv()
    make_probs(1)
    value_terms(1)
    drive(value_reduce(1), weights)
    settle(1)
    drive(col_gather(1), row_gather(1, key_all[0]), row_gather(2, value_all[1]))
    partials = spread_partials()
    make_probs(0)
    total = up[1].astype(F32) + own_share()
    for j, made in enumerate(partials, 1):
        made.wait_recv()
        total += part_in[j].astype(F32)
    results[1, 0] = total.astype(BF16)
    up[0] = results[1, 0]
    value_terms(0)
    deliver(1, 0)
    drive(value_reduce(0), chain(row_gather(3, value_all[0]), key_terms(1)))
    drive(last_projection(), key_reduce(1), chain(key_terms(0), key_reduce(0)))

    @pl.when(pipe == 0)
    def _():
        delivery(1, 0).wait_send()
        for j in (1, 2, 3):
            last_copy(j).wait_recv()
        for head in range(2):
            total = acc[:, lanes(2 * xpos + head)]
            for j in (1, 2, 3):
                total += last_in[j, head].astype(F32)
            input_out[:, lanes(head)] = total.astype(BF16)
        last_copy(2).wait_send()

    @pl.when(pipe == 1)
    def _():
        delivery(1, 0).wait_recv()
        input_out[:, other] = stage[0]
        for j in (1, 3):
            last_copy(j).wait_send()

    for kind in (1, 2):
        delivery(1, kind).wait_recv()
        outs[kind][:, other] = stage[kind]
        here_or_there(None, lambda section, kind=kind: delivery(section, kind).wait_send())

    @pl.when(jnp.logical_not(keep))
    def _():
        weight_move().wait_send()

    def swaps_left(section):
        for kind in range(2):
            for i in range(2):
                swap(kind, section, i).wait_send()

    here_or_there(swaps_left, None)
    for finish in finishing:
        finish()
    for made in sent:
        made.wait_send()


def body(grad_output, queries, keys, values, value_weight, random_table):
    rows = lax.axis_size("row")
    cols = lax.axis_size("col")
    tokens, features = grad_output.shape
    half = rows // 4
    ycount = cols // 2
    vmem = pl.BlockSpec(memory_space=pltpu.VMEM)
    hbm = pl.BlockSpec(memory_space=pl.ANY)
    dma = pltpu.SemaphoreType.DMA
    out = jax.ShapeDtypeStruct((tokens, features), BF16)
    tile = (BLOCK, HEAD_DIM)
    block = (tokens, HEAD_DIM)

    def run(*refs):
        kernel(rows, cols, *refs)

    flops = 10 * 2 * tokens * features * TILES * BLOCK + 2 * tokens * features * cols * features
    grads = pl.pallas_call(
        run,
        out_shape=(out, out, out),
        in_specs=[hbm] * 6,
        out_specs=(vmem, vmem, vmem),
        scratch_shapes=[
            pltpu.SMEM((random_table.size,), jnp.int32),
            pltpu.SMEM((random_table.size,), jnp.int32),
            *[pltpu.VMEM((2 * rows, *tile), BF16)] * 4,
            pltpu.VMEM((2, ycount, 4, HEAD_DIM, HEAD_DIM), BF16),
            pltpu.VMEM((2, 2 * ycount, *tile), BF16),
            pltpu.VMEM((2, *block), BF16),
            pltpu.VMEM((2, *block), BF16),
            pltpu.VMEM((2, QBLOCKS, BLOCK, TILES * BLOCK), F32),
            pltpu.VMEM((tokens, 4 * HEAD_DIM), F32),
            *[pltpu.VMEM((SLOTS, *tile), BF16)] * 8,
            pltpu.VMEM((4, 2, *tile), F32),
            pltpu.VMEM((4, 2, half, 2, *tile), BF16),
            pltpu.VMEM((4, 2, half, 2, *tile), BF16),
            pltpu.VMEM((2, 4, *block), BF16),
            pltpu.VMEM((4, *block), BF16),
            pltpu.VMEM((4, 2, *block), BF16),
            pltpu.VMEM((2, 3, *block), BF16),
            pltpu.VMEM((3, *block), BF16),
            dma((4, 2, half, 2)),
            dma((4, 2, half, 2)),
            dma((4, 2 * half)),
            dma((4, 2 * half)),
            dma((2, half, 2)),
            dma((2, half + 1, 2)),
            dma((half,)),
            dma((half,)),
            dma((2, 2, ycount // 2, 2)),
            dma((2, 2, ycount // 2, 2)),
            dma((4, 2, half, 2)),
            dma((4, 2, half, 2)),
            dma((14,)),
            dma((14,)),
            dma((2, 4)),
            dma((2, 4)),
            dma((7,)),
        ],
        compiler_params=pltpu.CompilerParams(
            collective_id=0, has_side_effects=True, vmem_limit_bytes=56 * 2**20
        ),
        cost_estimate=pl.CostEstimate(
            flops=flops, bytes_accessed=16 * tokens * features, transcendentals=0
        ),
        name="relay",
    )(
        random_table.reshape(-1),
        grad_output,
        queries[0],
        keys.reshape(2, BLOCK, features),
        values.reshape(2, BLOCK, features),
        value_weight.reshape(2, HEAD_DIM, HEAD_DIM),
    )
    return tuple(array[None] for array in grads)


def solution(mesh):
    in_specs = (
        P("row", "col"),
        P("pipe", "row", "col"),
        P("pipe", "row", "col"),
        P("pipe", "row", "col"),
        P("pipe", "col", "row"),
        P("pipe", None, "col", None),
    )
    out_specs = (P("pipe", "row", "col"), P("pipe", "row", "col"), P("pipe", "row", "col"))
    return jax.shard_map(body, mesh=mesh, in_specs=in_specs, out_specs=out_specs, check_vma=False)
```

time: 158 us -> 164 us (1.038)
  the two profiles are of different devices: /device:TPU:8 before, /device:TPU:4 now
where the time goes in v3:
time: 164 us
  Pallas kernels  159 us (97%)
  local copies, waits for them, and re-layouts  4.59 us (3%)
    pallas_call x1, Pallas kernels, body(): pl.pallas_call(run, out_shape=(out, out, out), in_specs=[hbm] * 6, out_sp...  159 us
    unnamed x10, local copies, waits for them, and re-layouts  3.79 us

profile of v3, /device:TPU:4, one launch (start us, length us, event | category | flops | bytes accessed | tf_op | source)
XLA Modules:
  0.0 164.2 jit_solution(11661898575097647813)
XLA Ops:
  0.6 0.0 copy-start.2
  0.6 0.7 copy-done.2
  1.3 0.1 copy.9
  1.4 0.8 reshape.18.refs_0_
  2.2 158.9 %relay.1 = (bf16[128,256]{1,0:T(8,128)(2,1)}, bf16[128,256]{1,0:T(8,128)(2,1)}, bf16[128,256]{1,0:T(8,128)(2,1)}) custom-call(s32[384]{0:T(512)} %reshape.18.refs_0_, bf16[128,256]{1,0:T(8,128)(2,1)} %refs_1_.1, bf16[128,256]{1,0:T(8,128)(2,1)} %bitcast.10, bf16[2,64,256]{2,1,0:T(8,128)(2,1)} %bitcast.11, bf16[2,64,256]{2,1,0:T(8,128)(2,1)} %bitcast.12, ...), custom_call_target="tpu_custom_call" | custom-call | flops 520093696 | bytes 524288 | tf_op jit(solution)/shard_map/relay/pallas_call | solution.py:752
  161.2 0.0 copy-start.1
  161.2 1.5 copy.13
  162.7 0.0 copy-done.1
  162.7 0.0 copy-start
  162.7 0.6 copy.14
  163.3 0.2 copy-done
  163.6 0.6 copy.15
Async XLA Ops:
  0.6 0.7 copy-start.2
  161.2 1.5 copy-start.1
  162.7 0.9 copy-start

commit v4 on v2

--- a/solution.py
+++ b/solution.py
@@ -44,6 +44,11 @@
     for i in range(0, half, 2):
         edges += [(i, j) for j in (i + 2, i + 1) if j <= half]
     return edges
+
+
+def chain(*streams):
+    for stream in streams:
+        yield from stream
 
 
 def lanes(head):
@@ -147,7 +152,7 @@
             device_id_type=MESH,
         )
 
-    def gather(sent, buf, pos, size, entry, device_at, skip, send, recv, shared=None, second=None, arrive=None):
+    def gather(sent, buf, pos, size, entry, device_at, skip, send, recv, shared=None, second=None, arrive=None, joined=False):
         half = size // 2
         edges = tree(half, skip)
 
@@ -156,6 +161,9 @@
 
         def copy(way, start, end, item, offset):
             block = ref(offset, item)
+            if joined and end < half:
+                place = lax.rem(pos + offset + size, size)
+                block = buf.at[pl.ds(entry(place, 0), 2)]
             return remote(
                 block,
                 block,
@@ -164,12 +172,33 @@
                 device_at(start - end if way else end - start),
             )
 
+        def push_all(distance):
+            for start, end in edges:
+                if start == distance:
+                    for way in range(2):
+                        made = copy(way, start, end, way, distance if way else -distance)
+                        made.start()
+                        sent.append(made)
+
         def push(way, distance, item):
             for start, end in edges:
                 if start == distance and (end < half or way == item):
                     made = copy(way, start, end, item, distance if way else -distance)
                     made.start()
                     sent.append(made)
+
+        if joined:
+            push_all(0)
+            shared(0)
+            yield
+            for start, end in edges:
+                for way in range(2):
+                    copy(way, start, end, way, end if way else -end).wait_recv()
+                push_all(end)
+                for offset in (-end, end)[: 2 if end < half else 1]:
+                    shared(offset)
+                yield
+            return
 
         for item in range(2):
             if item == 1 and second is not None:
@@ -223,6 +252,7 @@
             ring_send.at[which],
             ring_recv.at[which],
             shared=shared,
+            joined=True,
         )
         for made in shares:
             made.wait_recv()
@@ -342,19 +372,24 @@
 
         edges = tree(half, True)
 
-        def copy(way, start, end, part):
+        def copy(way, start, end):
+            parts = pl.ds(0, 2) if end < half else pl.ds(way, 1)
             return remote(
-                sbuf.at[way, end - 1, part],
-                rbuf.at[way, end - 1, part],
-                sum_send.at[which, way, end - 1, part],
-                sum_recv.at[which, way, end - 1, part],
+                sbuf.at[way, end - 1, parts],
+                rbuf.at[way, end - 1, parts],
+                sum_send.at[which, way, end - 1, 0],
+                sum_recv.at[which, way, end - 1, 0],
                 chip_at(start - end if way else end - start),
             )
+
+        def wait_for(way, distance):
+            for start, end in edges:
+                if start == distance:
+                    copy(way, start, end).wait_recv()
 
         def arrived(way, distance, part):
             for start, end in edges:
                 if start == distance and (end < half or way == part):
-                    copy(way, start, end, part).wait_recv()
                     yield rbuf[way, end - 1, part].astype(F32)
 
         exchange = remote(own, sib, one_send.at[which], one_recv.at[which], to_sibling)
@@ -362,20 +397,22 @@
         exchange.wait_recv()
         sent.append(exchange)
         for start, end in sorted(edges, key=lambda edge: (-edge[0], edge[1] % 2 == 0, -edge[1])):
-            for part in range(2):
-                for way in range(2):
-                    if end == half and part != way:
-                        continue
-                    total = contribution(-end if way else end, part)
+            for way in range(2):
+                parts = range(2) if end < half else [way]
+                totals = [contribution(-end if way else end, part) for part in parts]
+                wait_for(way, end)
+                for part, total in zip(parts, totals):
                     for term in arrived(way, end, part):
                         total += term
                     sbuf[way, end - 1, part] = total.astype(BF16)
-                    made = copy(way, start, end, part)
-                    made.start()
-                    sent.append(made)
-                yield
-        for part in range(2):
-            total = local[part] + contribution(0, part)
+                made = copy(way, start, end)
+                made.start()
+                sent.append(made)
+            yield
+        totals = [local[part] + contribution(0, part) for part in range(2)]
+        for way in range(2):
+            wait_for(way, 0)
+        for part, total in enumerate(totals):
             for way in range(2):
                 for term in arrived(way, 0, part):
                     total += term
@@ -451,7 +488,7 @@
         make_probs()
         value_terms()
         weights = row_gather(sent, 1, weight_all)
-        drive(value_reduce(sent), take(weights, 10, 4))
+        drive(value_reduce(sent), take(weights, 4, 3))
         acc[...] = up[...].astype(F32)
         drive(col_gather(sent, False), weights)
 
@@ -480,9 +517,10 @@
         drive(row_gather(sent, 1, weight_all), row_gather(sent, 2, value_all))
         upstream_copy().wait_recv()
         value_terms()
-        drive(value_reduce(sent), key_terms())
+        keys = chain(key_terms(), key_reduce(sent))
+        drive(value_reduce(sent), take(keys, 1, 7))
         acc[...] = up[...].astype(F32)
-        drive(col_gather(sent, True), key_reduce(sent))
+        drive(col_gather(sent, True), keys)
         input_out[...] = acc[...].astype(BF16)
         for made in sent:
             made.wait_send()

time: 158 us -> 153 us (0.968)
  Pallas kernels: 152 us -> 147 us
    pallas_call x1, Pallas kernels: 152 us -> 147 us  [body(): pl.pallas_call(run, out_shape=(out, out, out), in_specs=[pl.BlockSpec(mem...]
where the time goes in v4:
time: 153 us; the launch traced here: 152 us
  Pallas kernels  147 us (96%)
  local copies, waits for them, and re-layouts  4.59 us (3%)
    pallas_call x1, Pallas kernels, body(): pl.pallas_call(run, out_shape=(out, out, out), in_specs=[pl.BlockSpec(mem...  147 us
    unnamed x10, local copies, waits for them, and re-layouts  3.79 us

profile of v4, /device:TPU:8, one launch (start us, length us, event | category | flops | bytes accessed | tf_op | source)
XLA Modules:
  0.0 152.5 jit_solution(11328747254327975224)
XLA Ops:
  0.6 0.0 copy-start.2
  0.6 0.7 copy-done.2
  1.3 0.1 copy.9
  1.4 0.8 reshape.18.refs_0_
  2.2 147.2 %relay.1 = (bf16[128,256]{1,0:T(8,128)(2,1)}, bf16[128,256]{1,0:T(8,128)(2,1)}, bf16[128,256]{1,0:T(8,128)(2,1)}) custom-call(s32[384]{0:T(512)} %reshape.18.refs_0_, bf16[128,256]{1,0:T(8,128)(2,1)} %refs_1_.1, bf16[128,256]{1,0:T(8,128)(2,1)} %bitcast.10, bf16[2,64,256]{2,1,0:T(8,128)(2,1)} %bitcast.11, bf16[2,64,256]{2,1,0:T(8,128)(2,1)} %bitcast.12, ...), custom_call_target="tpu_custom_call" | custom-call | flops 520093696 | bytes 524288 | tf_op jit(solution)/shard_map/relay/pallas_call | solution.py:551
  149.5 0.0 copy-start.1
  149.5 1.5 copy.13
  151.0 0.0 copy-done.1
  151.0 0.0 copy-start
  151.0 0.6 copy.14
  151.6 0.2 copy-done
  151.8 0.6 copy.15
Async XLA Ops:
  0.6 0.7 copy-start.2
  149.5 1.5 copy-start.1
  151.0 0.9 copy-start
